TPU v7x, 32 devices: a whole 2x2x4 slice. The times are simulated.
32 devices in a mesh: grp: 2 (over y), seq: 4 (over z), head: 2 (over x), rep: 2 (over core).
Axes of the slice: x: 2, y: 2, z: 4, core: 2. Of those that a mesh axis runs over, the one named last changes fastest.
Arguments:
- tokens: bfloat16 [16, 2048, 4096], P(('grp', 'rep', 'head'), 'seq'), parts along dimension 0, may hold values from -250 to 250
- w_query: bfloat16 [4096, 2048], P(None, 'head'), may hold values from -0.09375 to 0.09375
- w_out: bfloat16 [2048, 4096], P('head'), may hold values from -0.5 to 0.5
- neighbour_kv: bfloat16 [256, 2, 128, 2048], P(('grp', 'seq', 'rep'), None, None, 'head'), parts along dimension 0, may hold values from -150 to 150
- shard_lists: int32 [16, 32, 2], P(('grp', 'seq', 'rep')), parts along dimension 0, may hold values from 0 to 3, as said below
- slot_lists: int32 [16, 32, 2], P(('grp', 'seq', 'rep')), parts along dimension 0, may hold values from 0 to 15
Outputs:
- crossed: bfloat16 [16, 2048, 4096], P(('grp', 'rep', 'head'), 'seq'), parts along dimension 0
There are 2 independent parts, one for each index of `grp`. A program takes and returns all parts, laid end to end along the dimension named above; an argument that names none is the same for every part. Nothing has to cross between parts.
Inputs may be any that keep to these rules, and one draw needn't show every extreme that they name: `shard_lists`: each entry row names 2 different encoder shards; at most 24 of the 64 entries of one owner name the same shard.
All inputs are finite; a program needn't handle non-finite values.
Results may differ from a plain program's by a relative error of at most 0.0038.
The roundings to bfloat16 on the way count: a program that leaves them out, or rounds other values in their place, can miss the bound.
Values may be sent and summed in bfloat16 or wider, within the bound.
A program may use at most 256 MiB of HBM per device.

v0:
```python
import jax
import jax.numpy as jnp
from jax import lax
from jax.sharding import PartitionSpec as P

DH = 128
BLOCK = 64
KN = 2


def body(tokens, w_query, w_out, neighbour_kv, shard_lists, slot_lists):
    local_seqs, local_span, feature_count = tokens.shape
    local_heads = w_query.shape[1] // DH
    widened = tokens.astype(jnp.float32)
    normed = (
        widened * lax.rsqrt(jnp.mean(widened * widened, axis=2, keepdims=True) + 1e-06)
    ).astype(jnp.bfloat16)
    product = jnp.einsum(
        "std,dh->sth",
        lax.all_gather(normed, "head", axis=0, tiled=True),
        w_query,
        preferred_element_type=jnp.float32,
    )
    queries = (product * DH ** (-0.5)).astype(jnp.bfloat16)
    seq_rep = queries.shape[0]
    own_blocks = seq_rep * local_span // BLOCK
    queries = queries.reshape(own_blocks, BLOCK, local_heads, DH)
    shards = shard_lists[0]
    slot_ids = slot_lists[0]
    store_count = neighbour_kv.shape[0]
    row_shape = neighbour_kv.shape[1:]
    neighbour_rows = row_shape[1]
    wanted = shards * store_count + slot_ids
    blank_rows = jnp.zeros((own_blocks, KN) + row_shape, jnp.bfloat16)
    pieces = lax.all_gather(neighbour_kv, "seq", axis=0, tiled=True)
    inside = (wanted >= 0) & (wanted < pieces.shape[0])
    clipped = jnp.clip(wanted, 0, pieces.shape[0] - 1).reshape(-1)
    picked_rows = jnp.take(pieces, clipped, axis=0).reshape(blank_rows.shape)
    fetched = jnp.where(inside[:, :, None, None, None], picked_rows, blank_rows)
    key_rows = fetched[:, :, 0].reshape(own_blocks, KN * neighbour_rows, local_heads, DH)
    value_rows = fetched[:, :, 1].reshape(own_blocks, KN * neighbour_rows, local_heads, DH)
    scores = jnp.einsum("oqhd,okhd->ohqk", queries, key_rows, preferred_element_type=jnp.float32)
    weights = jax.nn.softmax(scores, axis=-1).astype(jnp.bfloat16)
    context = jnp.einsum(
        "ohqk,okhd->oqhd", weights, value_rows, preferred_element_type=jnp.float32
    ).astype(jnp.bfloat16)
    context = context.reshape(seq_rep, local_span, local_heads * DH)
    return lax.psum_scatter(
        jnp.einsum("sth,hd->std", context, w_out, preferred_element_type=jnp.float32).astype(
            jnp.bfloat16
        ),
        "head",
        scatter_dimension=0,
        tiled=True,
    )


def solution(mesh):
    placed = (
        P(("grp", "rep", "head"), "seq", None),
        P(None, "head"),
        P("head", None),
        P(("grp", "seq", "rep"), None, None, "head"),
        P(("grp", "seq", "rep"), None, None),
        P(("grp", "seq", "rep"), None, None),
    )
    return jax.shard_map(
        body,
        mesh=mesh,
        in_specs=placed,
        out_specs=P(("grp", "rep", "head"), "seq", None),
        check_vma=False,
    )
```

profile of v0, /device:TPU:0, one launch (start us, length us, event | category | flops | bytes accessed | tf_op | source)
XLA Modules:
  0.0 1136.3 jit_solution(1778182654640954859)
XLA Ops:
  6.5 0.0 all-gather.5.cloned.1.call-start
  6.5 5.1 fusion.2
  11.6 0.0 copy-start
  11.6 0.0 copy-start.1
  11.7 10.2 fusion.3
  21.8 0.0 all-gather.5.cloned.1.call-update
  21.8 0.0 all-gather.3.cloned.1.call-start
  21.9 0.7 all-gather.3.cloned.1.call-update
  22.6 0.2 reduce-scatter.2.cloned.1.call-start
  22.8 0.0 copy-done
  22.8 0.0 copy-done.1
  22.9 0.1 copy.21
  22.9 0.1 min.18
  23.0 0.1 copy.20
  23.2 0.1 copy.19
  23.3 200.3 %all-gather.5.cloned.1.call-done = bf16[4,512,4096]{2,1,0:T(8,128)(2,1)} async-done(((bf16[2,512,4096]{2,1,0:T(8,128)(2,1)}), bf16[4,512,4096]{2,1,0:T(8,128)(2,1)}) %all-gather.5.cloned.1.call-update) | async-done | bytes 16777232 | tf_op jit(solution)/shard_map/all_gather | solution.py:20
  223.5 22.7 %multiply_convert_fusion = bf16[4,512,1024]{2,1,0:T(8,128)(2,1)S(1)} fusion(bf16[4,512,4096]{2,1,0:T(8,128)(2,1)} %all-gather.5.cloned.1.call-done, bf16[4096,1024]{1,0:T(8,128)(2,1)} %param.7), kind=kOutput, calls=%fused_computation.19 | convolution fusion | flops 17184063488 | bytes 29360128 | tf_op jit(solution)/shard_map/std,dh->sth/dot_general | solution.py:18
  246.2 3.1 copy.27
  249.3 537.2 %all-gather.3.cloned.1.call-done = bf16[64,2,128,1024]{3,2,1,0:T(8,128)(2,1)} async-done(((bf16[16,2,128,1024]{3,2,1,0:T(8,128)(2,1)}), bf16[64,2,128,1024]{3,2,1,0:T(8,128)(2,1)}) %all-gather.3.cloned.1.call-update) | async-done | bytes 33554448 | tf_op jit(solution)/shard_map/all_gather | solution.py:35
  786.6 22.7 %gather_fusion = bf16[64,2,128,1024]{3,2,1,0:T(8,128)(2,1)} fusion(bf16[64,2,128,1024]{3,2,1,0:T(8,128)(2,1)} %all-gather.3.cloned.1.call-done, s32[1024]{0:T(1024)S(1)} %pad_clamp_fusion), kind=kCustom, calls=%fused_computation | custom fusion | bytes 67109120 | tf_op jit(solution)/shard_map/jit(_take)/gather | solution.py:38
  809.2 22.9 %fusion.1 = bf16[32,2,2,128,1024]{4,3,1,0,2:T(8,128)(2,1)} fusion(bf16[32,2,2,128,1024]{4,3,2,1,0:T(8,128)(2,1)} %bitcast.37, pred[32,2]{1,0:T(8,128)(4,1)S(1)} %copy.20, pred[32,2]{1,0:T(8,128)(4,1)S(1)} %copy.19), kind=kLoop, calls=%fused_computation.3 | loop fusion | flops 33554432 | bytes 67108992 | tf_op jit(solution)/shard_map/jit(_where)/select_n | solution.py:39
  832.1 12.8 %fusion.18 = (bf16[32,2,1,128,1024]{4,3,1,0,2:T(8,128)(2,1)S(1)}, bf16[32,2,1,128,1024]{4,3,1,0,2:T(8,128)(2,1)S(1)}) fusion(bf16[32,2,2,128,1024]{4,3,1,0,2:T(8,128)(2,1)} %fusion.1), kind=kLoop, calls=%fused_computation.31 | loop fusion | bytes 67108864 | tf_op jit(solution)/shard_map/slice | solution.py:40
  844.9 9.1 copy.28
  854.1 9.1 copy.29
  863.1 17.5 %fusion.19 = (f32[32,8,64]{2,1,0:T(8,128)S(1)}, f32[32,8,64,256]{3,2,1,0:T(8,128)}) fusion(bf16[32,256,8,128]{3,2,1,0:T(8,128)(2,1)} %bitcast.38, bf16[32,64,8,128]{3,2,1,0:T(8,128)(2,1)} %bitcast.41), kind=kOutput, calls=%fused_computation.32 | convolution fusion | flops 1082130688 | bytes 37814272 | tf_op jit(solution)/shard_map/sub | solution.py:43
  880.7 15.7 %convert_bitcast_fusion = bf16[32,64,8,128]{3,1,2,0:T(8,128)(2,1)} fusion(bf16[32,256,8,128]{3,2,1,0:T(8,128)(2,1)} %bitcast.42, f32[32,8,64,256]{3,2,1,0:T(8,128)} %get-tuple-element.10, f32[32,8,64]{2,1,0:T(8,128)S(1)} %get-tuple-element.9), kind=kOutput, calls=%fused_computation.21 | convolution fusion | flops 1084227584 | bytes 37814272 | tf_op jit(solution)/shard_map/ohqk,okhd->oqhd/dot_general | solution.py:44
  896.3 12.3 %copy.26 = bf16[32,64,8,128]{3,2,1,0:T(8,128)(2,1)} copy(bf16[32,64,8,128]{3,1,2,0:T(8,128)(2,1)} %convert_bitcast_fusion) | data formatting | bytes 8388608 | tf_op jit(solution)/shard_map/convert_element_type | solution.py:46
  908.6 7.3 reshape.95
  915.9 24.6 %convolution_convert_fusion = bf16[4,512,4096]{2,1,0:T(8,128)(2,1)} fusion(bf16[4,512,1024]{2,1,0:T(8,128)(2,1)} %reshape.95, bf16[1024,4096]{1,0:T(8,128)(2,1)} %param.8), kind=kOutput, calls=%fused_computation.14 | convolution fusion | flops 17188257792 | bytes 29360128 | tf_op jit(solution)/shard_map/sth,hd->std/dot_general | solution.py:49
  940.4 0.0 reduce-scatter.2.cloned.1.call-update
  940.5 189.3 %reduce-scatter.2.cloned.1.call-done = bf16[2,512,4096]{2,1,0:T(8,128)(2,1)} async-done(((bf16[4,512,4096]{2,1,0:T(8,128)(2,1)}), bf16[2,512,4096]{2,1,0:T(8,128)(2,1)}) %reduce-scatter.2.cloned.1.call-update) | async-done | bytes 8388624 | tf_op jit(solution)/shard_map/reduce_scatter | solution.py:48
  (5 shorter events, 0.0 us)
Async XLA Ops:
  6.5 217.0 %all-gather.5.cloned.1.call-start = ((), (), s32[]{:S(2)}) async-start(), calls=%async_computation.2 | async-start | bytes 25165824 | tf_op jit(solution)/shard_map/all_gather | solution.py:20
  11.6 11.2 copy-start
  11.6 11.2 copy-start.1
  21.8 764.7 %all-gather.3.cloned.1.call-start = ((), (), s32[]{:S(2)}) async-start(), calls=%async_computation.1 | async-start | bytes 41943040 | tf_op jit(solution)/shard_map/all_gather | solution.py:35
  22.6 1107.2 %reduce-scatter.2.cloned.1.call-start = ((), (), s32[]{:S(2)}) async-start(), calls=%async_computation.3 | async-start | bytes 25165824 | tf_op jit(solution)/shard_map/reduce_scatter | solution.py:48
Sparse Core Ops, SparseCore 0:
  22.0 201.5 all-gather.4
  225.1 561.3 all-gather.2
  940.6 189.1 reduce-scatter.1
where the time goes:
time: 1140 us
  waiting for transfers between devices  928 us (81%)
  matrix products  80.4 us (7%)
  local copies, waits for them, and re-layouts  76.7 us (7%)
  other arithmetic  38.2 us (3%)
  between operations  13.2 us (1%)
    all_gather x1, waiting for transfers between devices, body(): pieces = lax.all_gather(neighbour_kv, 'seq', axis=0, tiled=True)  537 us
    all_gather x1, waiting for transfers between devices, body(): lax.all_gather(normed, 'head', axis=0, tiled=True)  200 us
    reduce_scatter x1, waiting for transfers between devices, body(): lax.psum_scatter(jnp.einsum('sth,hd->std', context, w_out, preferred_elem...  189 us
    dot_general x1, matrix products, body(): jnp.einsum('sth,hd->std', context, w_out, preferred_element_type=jnp.floa...  24.6 us
    select_n x1, other arithmetic, body(): fetched = jnp.where(inside[:, :, None, None, None], picked_rows, blank_rows)  22.9 us
  transfers between devices with their start and end apart: 3, of which 3 were waited for; matrix products, arithmetic and copies ran while one was open for 2% of the time, Pallas kernels for 0%

commit v1 on v0

v1 whole, which is shorter than its diff:
```python
import functools

import jax
import jax.numpy as jnp
from jax import lax
from jax.experimental import pallas as pl
from jax.experimental.pallas import tpu as pltpu
from jax.sharding import PartitionSpec as P

DH = 128
BLOCK = 64
KN = 2


def plain_body(tokens, w_query, w_out, neighbour_kv, shard_lists, slot_lists):
    local_seqs, local_span, feature_count = tokens.shape
    local_heads = w_query.shape[1] // DH
    widened = tokens.astype(jnp.float32)
    normed = (
        widened * lax.rsqrt(jnp.mean(widened * widened, axis=2, keepdims=True) + 1e-06)
    ).astype(jnp.bfloat16)
    product = jnp.einsum(
        "std,dh->sth",
        lax.all_gather(normed, "head", axis=0, tiled=True),
        w_query,
        preferred_element_type=jnp.float32,
    )
    queries = (product * DH ** (-0.5)).astype(jnp.bfloat16)
    seq_rep = queries.shape[0]
    own_blocks = seq_rep * local_span // BLOCK
    queries = queries.reshape(own_blocks, BLOCK, local_heads, DH)
    store_count = neighbour_kv.shape[0]
    row_shape = neighbour_kv.shape[1:]
    wanted = shard_lists[0] * store_count + slot_lists[0]
    pieces = lax.all_gather(neighbour_kv, "seq", axis=0, tiled=True)
    fetched = jnp.take(pieces, wanted.reshape(-1), axis=0).reshape((own_blocks, KN) + row_shape)
    key_rows = fetched[:, :, 0].reshape(own_blocks, KN * row_shape[1], local_heads, DH)
    value_rows = fetched[:, :, 1].reshape(own_blocks, KN * row_shape[1], local_heads, DH)
    scores = jnp.einsum("oqhd,okhd->ohqk", queries, key_rows, preferred_element_type=jnp.float32)
    weights = jax.nn.softmax(scores, axis=-1).astype(jnp.bfloat16)
    context = jnp.einsum(
        "ohqk,okhd->oqhd", weights, value_rows, preferred_element_type=jnp.float32
    ).astype(jnp.bfloat16)
    context = context.reshape(seq_rep, local_span, local_heads * DH)
    return lax.psum_scatter(
        jnp.einsum("sth,hd->std", context, w_out, preferred_element_type=jnp.float32).astype(
            jnp.bfloat16
        ),
        "head",
        scatter_dimension=0,
        tiled=True,
    )


def attend_kernel(n_kv, n_q, picks_ref, *refs):
    kv_refs = refs[:n_kv]
    q_refs = refs[n_kv:n_kv + n_q]
    o_refs = refs[n_kv + n_q:n_kv + 2 * n_q]
    store, sems = refs[n_kv + 2 * n_q:]
    count = kv_refs[0].shape[0]
    copies = [
        pltpu.make_async_copy(kv_refs[k], store.at[pl.ds(k * count, count)], sems.at[k])
        for k in range(n_kv)
    ]
    for copy in copies:
        copy.start()
    for copy in copies:
        copy.wait()
    rows, width = q_refs[0].shape
    blocks = rows // BLOCK
    heads = width // DH
    blank = jnp.zeros((BLOCK, DH), jnp.bfloat16)

    for piece in range(n_q):
        q_ref, o_ref = q_refs[piece], o_refs[piece]

        def step(block, carry, q_ref=q_ref, o_ref=o_ref, piece=piece):
            at = (piece * blocks + block) * KN
            chosen = [picks_ref[at + k] for k in range(KN)]
            keys = jnp.concatenate([store[i, 0] for i in chosen], axis=0)
            values = jnp.concatenate([store[i, 1] for i in chosen], axis=0)
            span = pl.ds(pl.multiple_of(block * BLOCK, BLOCK), BLOCK)
            q = q_ref[span, :]
            spread = jnp.concatenate(
                [
                    jnp.concatenate(
                        [q[:, h * DH:(h + 1) * DH] if h == g else blank for h in range(heads)], axis=1
                    )
                    for g in range(heads)
                ],
                axis=0,
            )
            scores = lax.dot_general(
                spread, keys, (((1,), (1,)), ((), ())), preferred_element_type=jnp.float32
            )
            grown = jnp.exp(scores - jnp.max(scores, axis=-1, keepdims=True))
            weights = (grown / jnp.sum(grown, axis=-1, keepdims=True)).astype(jnp.bfloat16)
            mixed = jnp.dot(weights, values, preferred_element_type=jnp.float32)
            o_ref[span, :] = jnp.concatenate(
                [mixed[h * BLOCK:(h + 1) * BLOCK, h * DH:(h + 1) * DH] for h in range(heads)], axis=1
            ).astype(jnp.bfloat16)
            return carry

        lax.fori_loop(0, blocks, step, 0, unroll=4 if blocks % 4 == 0 else 1)


def attend(picks, kv_pieces, q_pieces):
    n_kv, n_q = len(kv_pieces), len(q_pieces)
    count = kv_pieces[0].shape[0]
    whole = pl.BlockSpec(memory_space=pltpu.VMEM)
    return pl.pallas_call(
        functools.partial(attend_kernel, n_kv, n_q),
        out_shape=[jax.ShapeDtypeStruct(q.shape, q.dtype) for q in q_pieces],
        in_specs=[pl.BlockSpec(memory_space=pltpu.SMEM)]
        + [pl.BlockSpec(memory_space=pl.ANY)] * n_kv
        + [whole] * n_q,
        out_specs=[whole] * n_q,
        scratch_shapes=[
            pltpu.VMEM((n_kv * count,) + kv_pieces[0].shape[1:], jnp.bfloat16),
            pltpu.SemaphoreType.DMA((n_kv,)),
        ],
        compiler_params=pltpu.CompilerParams(vmem_limit_bytes=48 * 2**20),
        name="attend",
    )(picks, *kv_pieces, *q_pieces)


def spread_body(n_seq, n_head, tokens, w_query, w_out, neighbour_kv, shard_lists, slot_lists):
    s = lax.axis_index("seq")
    x = lax.axis_index("head")
    r = lax.axis_index("rep")
    local_seqs, local_span, features = tokens.shape
    rows = local_seqs * local_span
    local_width = w_query.shape[1]
    width = local_width // n_seq
    store_count = neighbour_kv.shape[0]
    flip = [(0, 1), (1, 0)]

    def send(array, dz, dx):
        order = []
        for a in range(n_seq):
            for b in range(n_head):
                order.append((a * n_head + b, (a + dz) % n_seq * n_head + (b + dx) % n_head))
        return lax.ppermute(array, ("seq", "head"), order)

    def columns(array, dz):
        at = lax.rem(s + dz, n_seq) * width
        return lax.dynamic_slice_in_dim(array, at, width, axis=array.ndim - 1)

    def other_half(w, axis):
        half = w.shape[axis] // 2
        mine = lax.dynamic_slice_in_dim(w, r * half, half, axis=axis)
        first = lax.ppermute(mine, "head", flip)
        second = lax.ppermute(first, "rep", flip)
        low = jnp.where(r == 0, first, second)
        high = jnp.where(r == 0, second, first)
        return jnp.concatenate([low, high], axis=axis)

    kv_pieces = [columns(neighbour_kv, 0)]
    for dz in range(1, n_seq):
        kv_pieces.append(send(columns(neighbour_kv, dz), dz, 0))

    w_query_other = other_half(w_query, 0)
    w_out_other = other_half(w_out, 0)

    lists = jnp.stack([shard_lists[0], slot_lists[0]])
    gathered = lax.all_gather(lists, "seq", axis=0)
    places = lax.rem(s - gathered[:, 0] + n_seq, n_seq) * store_count + gathered[:, 1]
    places = places.reshape(n_seq, n_head, -1)
    picks = []
    for dz in range(n_seq):
        for dx in range(n_head):
            picks.append(places[lax.rem(s - dz + n_seq, n_seq), lax.rem(x - dx + n_head, n_head)])
    picks = jnp.concatenate(picks).astype(jnp.int32)

    widened = tokens.reshape(rows, features).astype(jnp.float32)
    normed = (
        widened * lax.rsqrt(jnp.mean(widened * widened, axis=1, keepdims=True) + 1e-06)
    ).astype(jnp.bfloat16)

    def project(w):
        product = jnp.dot(normed, w, preferred_element_type=jnp.float32)
        return (product * DH ** (-0.5)).astype(jnp.bfloat16)

    queries = [project(w_query), project(w_query_other)]
    q_pieces = []
    for dz in range(n_seq):
        for dx in range(n_head):
            piece = columns(queries[dx], dz)
            q_pieces.append(piece if dz == dx == 0 else send(piece, dz, dx))

    c_pieces = attend(picks, kv_pieces, q_pieces)

    back = [[None] * n_seq for _ in range(n_head)]
    for dz in range(n_seq):
        for dx in range(n_head):
            piece = c_pieces[dz * n_head + dx]
            back[dx][dz] = piece if dz == dx == 0 else send(piece, -dz, -dx)
    terms = []
    for dx, w in enumerate([w_out, w_out_other]):
        twice = jnp.concatenate(back[dx] + back[dx], axis=1)
        context = lax.dynamic_slice_in_dim(
            twice, lax.rem(n_seq - s, n_seq) * width, local_width, axis=1
        )
        terms.append(jnp.dot(context, w, preferred_element_type=jnp.float32).astype(jnp.bfloat16))
    crossed = (terms[0].astype(jnp.float32) + terms[1].astype(jnp.float32)).astype(jnp.bfloat16)
    return crossed.reshape(local_seqs, local_span, w_out.shape[1])


def solution(mesh):
    placed = (
        P(("grp", "rep", "head"), "seq", None),
        P(None, "head"),
        P("head", None),
        P(("grp", "seq", "rep"), None, None, "head"),
        P(("grp", "seq", "rep"), None, None),
        P(("grp", "seq", "rep"), None, None),
    )
    sizes = dict(mesh.shape)
    n_seq, n_head = sizes["seq"], sizes["head"]

    def body(*arrays):
        local_heads = arrays[1].shape[1] // DH
        if n_head == 2 and sizes["rep"] == 2 and local_heads % n_seq == 0:
            return spread_body(n_seq, n_head, *arrays)
        return plain_body(*arrays)

    return jax.shard_map(
        body,
        mesh=mesh,
        in_specs=placed,
        out_specs=P(("grp", "rep", "head"), "seq", None),
        check_vma=False,
    )
```

time: 1140 us -> 654 us (0.57)
  waiting for transfers between devices: 928 us -> 333 us
  blocking collectives: 0 us -> 79.2 us
  starting transfers between devices: 0.26 us -> 78.7 us
  Pallas kernels: 0 us -> 58.5 us
  local copies, waits for them, and re-layouts: 76.7 us -> 32.8 us
  matrix products: 80.4 us -> 50.3 us
  other arithmetic: 38.2 us -> 20.5 us
  between operations: 13.2 us -> 0.36 us
    all_gather x2 -> x0, waiting for transfers between devices: 737 us -> none  [the longest x1 537 us: body(): pieces = lax.all_gather(neighbour_kv, 'seq', axis=0, tiled=True)]
    ppermute x0 -> x21, waiting for transfers between devices: none -> 333 us  [the longest x17 184 us: send(): return lax.ppermute(array, ('seq', 'head'), order)]
    reduce_scatter x1 -> x0, waiting for transfers between devices: 189 us -> none  [body(): lax.psum_scatter(jnp.einsum('sth,hd->std', context, w_out, preferred_elem...]
    all_gather x0 -> x1, blocking collectives: none -> 79.2 us  [spread_body(): gathered = lax.all_gather(lists, 'seq', axis=0)]
    ppermute x0 -> x21, starting transfers between devices: none -> 78.7 us  [the longest x17 75.8 us: send(): return lax.ppermute(array, ('seq', 'head'), order)]
    pallas_call x0 -> x1, Pallas kernels: none -> 58.5 us  [attend(): pl.pallas_call(functools.partial(attend_kernel, n_kv, n_q), out_shape=[ja...]
    gather x1 -> x0, local copies, waits for them, and re-layouts: 22.7 us -> none  [body(): picked_rows = jnp.take(pieces, clipped, axis=0).reshape(blank_rows.shape)]
    dynamic_slice x0 -> x6, local copies, waits for them, and re-layouts: none -> 21.2 us  [the longest x3 11.2 us: columns(): return lax.dynamic_slice_in_dim(array, at, width, axis=array.ndim - 1)]
  transfers between devices with their start and end apart: 3 -> 21, of which waited for: 3 -> 9; matrix products, arithmetic and copies ran while one was open for 2% -> 12% of each run, Pallas kernels for 0% -> 9%
where the time goes in v1:
time: 654 us; the launch traced here: 653 us
  waiting for transfers between devices  333 us (51%)
  blocking collectives  79.2 us (12%)
  starting transfers between devices  78.7 us (12%)
  Pallas kernels  58.5 us (9%)
  matrix products  50.3 us (8%)
  local copies, waits for them, and re-layouts  32.8 us (5%)
  other arithmetic  20.5 us (3%)
    ppermute x17, waiting for transfers between devices, send(): return lax.ppermute(array, ('seq', 'head'), order)  184 us
    ppermute x2, waiting for transfers between devices, other_half(): first = lax.ppermute(mine, 'head', flip)  149 us
    all_gather x1, blocking collectives, spread_body(): gathered = lax.all_gather(lists, 'seq', axis=0)  79.2 us
    ppermute x17, starting transfers between devices, send(): return lax.ppermute(array, ('seq', 'head'), order)  75.8 us
    pallas_call x1, Pallas kernels, attend(): pl.pallas_call(functools.partial(attend_kernel, n_kv, n_q), out_shape=[ja...  58.5 us
    dot_general x2, matrix products, spread_body(): jnp.dot(context, w, preferred_element_type=jnp.float32).astype(jnp.bfloat16)  26.6 us
    dot_general x2, matrix products, project(): product = jnp.dot(normed, w, preferred_element_type=jnp.float32)  23.6 us
  transfers between devices with their start and end apart: 21, of which 9 were waited for; matrix products, arithmetic and copies ran while one was open for 12% of the time, Pallas kernels for 9%

profile of v1, /device:TPU:0, one launch (start us, length us, event | category | flops | bytes accessed | tf_op | source)
XLA Modules:
  0.0 653.3 jit_solution(4886625747117890035)
XLA Ops:
  0.0 4.6 constant_dynamic-slice_fusion.8
  4.6 2.9 collective-permute-start.3
  7.6 5.0 constant_dynamic-slice_fusion
  12.6 1.2 copy-done
  13.7 1.7 multiply_reduce_fusion
  15.4 83.9 %collective-permute-done.3 = bf16[2048,1024]{1,0:T(8,128)(2,1)} collective-permute-done((bf16[2048,1024]{1,0:T(8,128)(2,1)}, bf16[2048,1024]{1,0:T(8,128)(2,1)}, u32[]{:S(2)}, u32[]{:S(2)}) %collective-permute-start.3) | collective-permute-done | bytes 4194336 | tf_op jit(solution)/shard_map/ppermute | solution.py:152
  99.4 10.1 %fusion = bf16[1024,4096]{1,0:T(8,128)(2,1)} fusion(f32[1024]{0:T(1024)S(1)} %bitcast.22, bf16[2,512,4096]{2,1,0:T(8,128)(2,1)} %param.6), kind=kLoop, calls=%fused_computation.1 | loop fusion | flops 12582912 | bytes 16781312 | tf_op jit(solution)/shard_map/convert_element_type | solution.py:178
  109.5 13.7 %multiply_convert_fusion.1 = bf16[1024,1024]{1,0:T(8,128)(2,1)S(1)} fusion(bf16[1024,4096]{1,0:T(8,128)(2,1)} %fusion, bf16[4096,1024]{1,0:T(8,128)(2,1)} %param.7), kind=kOutput, calls=%fused_computation.13 | convolution fusion | flops 8592031744 | bytes 18874368 | tf_op jit(solution)/shard_map/dot_general | solution.py:181
  123.2 65.2 %collective-permute-done.19 = bf16[512,4096]{1,0:T(8,128)(2,1)} collective-permute-done((bf16[512,4096]{1,0:T(8,128)(2,1)}, bf16[512,4096]{1,0:T(8,128)(2,1)}, u32[]{:S(2)}, u32[]{:S(2)}) %collective-permute-start.19) | collective-permute-done | bytes 4194336 | tf_op jit(solution)/shard_map/ppermute | solution.py:152
  188.3 1.2 constant_dynamic-slice_fusion.2
  189.6 3.9 collective-permute-start.10
  193.4 7.1 %constant_dynamic-slice_fusion.10 = (bf16[16,2,128,256]{3,2,1,0:T(8,128)(2,1)}, bf16[16,2,128,256]{3,2,1,0:T(8,128)(2,1)}, bf16[16,2,128,256]{3,2,1,0:T(8,128)(2,1)}, bf16[16,2,128,256]{3,2,1,0:T(8,128)(2,1)}) fusion(bf16[16,2,128,1024]{3,2,1,0:T(8,128)(2,1)} %param.9, s32[]{:T(128)S(6)} %select_n.91, s32[]{:T(128)S(6)} %select_n.89, s32[]{:T(128)S(6)} %select_n.88, ...), kind=kLoop, calls=%fused_computation.63 | loop fusion | bytes 16777232 | tf_op jit(solution)/shard_map/dynamic_slice | solution.py:147
  200.6 0.5 collective-permute-start.2
  201.1 79.2 %all-gather = s32[8,32,2]{1,2,0:T(2,128)S(1)} all-gather(s32[2,32,2]{1,2,0:T(2,128)S(1)} %pad_add_fusion), channel_id=2, replica_groups=mesh['grp'=2,'seq'=4,'head'=2,'rep'=2] {'seq'}, dimensions={0}, use_global_device_ids=true | all-gather | bytes 2560 | tf_op jit(solution)/shard_map/all_gather | solution.py:166
  280.4 0.0 collective-permute-start
  280.4 0.0 slice-start.1
  280.4 0.4 collective-permute-start.1
  280.8 4.1 broadcast_select_fusion.3
  284.9 3.9 collective-permute-start.6
  288.9 10.0 %multiply_convert_fusion = bf16[1024,1024]{1,0:T(8,128)(2,1)} fusion(bf16[1024,4096]{1,0:T(8,128)(2,1)S(1)} %bitcast.16, bf16[2048,1024]{1,0:T(8,128)(2,1)S(1)} %get-tuple-element.32, bf16[2048,1024]{1,0:T(8,128)(2,1)S(1)} %get-tuple-element.31), kind=kOutput, calls=%fused_computation.12 | convolution fusion | flops 8608808960 | bytes 18874368 | tf_op jit(solution)/shard_map/dot_general | solution.py:181
  298.8 2.9 constant_dynamic-slice_fusion.1
  301.7 81.9 %collective-permute-done.6.refs_6_ = bf16[1024,256]{1,0:T(8,128)(2,1)S(1)} collective-permute-done((bf16[1024,256]{1,0:T(8,128)(2,1)S(1)}, bf16[1024,256]{1,0:T(8,128)(2,1)S(1)}, u32[]{:S(2)}, u32[]{:S(2)}) %collective-permute-start.6) | collective-permute-done | bytes 524320 | tf_op jit(solution)/shard_map/ppermute | solution.py:143
  383.6 0.4 collective-permute-start.11
  384.0 54.5 %collective-permute-start.9 = (bf16[1024,256]{1,0:T(8,128)(2,1)}, bf16[1024,256]{1,0:T(8,128)(2,1)}, u32[]{:S(2)}, u32[]{:S(2)}) collective-permute-start(bf16[1024,256]{1,0:T(8,128)(2,1)} %get-tuple-element.38), channel_id=1, source_target_pairs={{0,10},{2,8},{4,14},{6,12},{8,2},{10,0},{12,6},{14,4},{1,11},{3,9}... | collective-permute-start | bytes 1572872 | tf_op jit(solution)/shard_map/ppermute | solution.py:143
  438.5 2.9 collective-permute-start.7
  441.3 0.6 collective-permute-start.5
  441.9 0.7 copy-done.3
  442.7 0.1 copy.15
  442.8 0.1 copy.16
  443.0 0.3 dynamic-slice_reduce_fusion
  443.3 0.1 concatenate.15.picks_ref
  443.4 4.4 collective-permute-done.11.refs_11_
  447.8 17.2 %collective-permute-done.9.refs_9_ = bf16[1024,256]{1,0:T(8,128)(2,1)} collective-permute-done((bf16[1024,256]{1,0:T(8,128)(2,1)}, bf16[1024,256]{1,0:T(8,128)(2,1)}, u32[]{:S(2)}, u32[]{:S(2)}) %collective-permute-start.9) | collective-permute-done | bytes 524320 | tf_op jit(solution)/shard_map/ppermute | solution.py:143
  465.0 17.7 %collective-permute-done.7.refs_7_ = bf16[1024,256]{1,0:T(8,128)(2,1)} collective-permute-done((bf16[1024,256]{1,0:T(8,128)(2,1)}, bf16[1024,256]{1,0:T(8,128)(2,1)}, u32[]{:S(2)}, u32[]{:S(2)}) %collective-permute-start.7) | collective-permute-done | bytes 524320 | tf_op jit(solution)/shard_map/ppermute | solution.py:143
  482.8 58.5 %attend.1 = (bf16[1024,256]{1,0:T(8,128)(2,1)S(1)}, bf16[1024,256]{1,0:T(8,128)(2,1)S(1)}, bf16[1024,256]{1,0:T(8,128)(2,1)S(1)}, bf16[1024,256]{1,0:T(8,128)(2,...) custom-call(s32[256]{0:T(256)S(1)} %concatenate.15.picks_ref, ...), custom_call_target="tpu_custom_call" | custom-call | tf_op jit(solution)/shard_map/attend/pallas_call | solution.py:111
  541.3 0.1 collective-permute-start.12
  541.4 0.4 collective-permute-start.13
  541.8 1.7 collective-permute-start.14
  543.5 4.5 broadcast_select_fusion.1
  548.0 1.6 collective-permute-start.15
  549.6 1.6 collective-permute-start.16
  551.2 0.9 constant_dynamic-update-slice_fusion.7
  552.1 1.7 collective-permute-done.12
  553.8 3.3 collective-permute-start.17
  557.2 0.9 constant_dynamic-update-slice_fusion.6
  558.1 30.2 %collective-permute-done.13 = bf16[1024,256]{1,0:T(8,128)(2,1)S(1)} collective-permute-done((bf16[1024,256]{1,0:T(8,128)(2,1)S(1)}, bf16[1024,256]{1,0:T(8,128)(2,1)S(1)}, u32[]{:S(2)}, u32[]{:S(2)}) %collective-permute-start.13) | collective-permute-done | bytes 524320 | tf_op jit(solution)/shard_map/ppermute | solution.py:143
  588.3 0.8 constant_dynamic-update-slice_fusion.5
  589.1 0.9 constant_dynamic-update-slice_fusion.4
  590.0 0.8 constant_dynamic-update-slice_fusion.3
  590.8 0.9 constant_dynamic-update-slice_fusion.2
  591.7 0.9 constant_dynamic-update-slice_fusion.1
  592.6 0.9 constant_dynamic-update-slice_fusion
  593.4 12.6 %fusion.14 = bf16[1024,4096]{1,0:T(8,128)(2,1)} fusion(bf16[1024,4096]{1,0:T(8,128)(2,1)S(1)} %bitcast.18, bf16[1024,2048]{1,0:T(8,128)(2,1)} %constant_dynamic-update-slice_fusion, s32[]{:T(128)S(6)} %select_n.96), kind=kOutput, calls=%fused_computation.19 | convolution fusion | flops 8589934592 | bytes 18874372 | tf_op jit(solution)/shard_map/dot_general | solution.py:204
  606.1 0.1 constant_dynamic-update-slice_fusion.15
  606.2 0.1 constant_dynamic-update-slice_fusion.14
  606.2 30.7 %collective-permute-done.17 = bf16[1024,256]{1,0:T(8,128)(2,1)S(1)} collective-permute-done((bf16[1024,256]{1,0:T(8,128)(2,1)S(1)}, bf16[1024,256]{1,0:T(8,128)(2,1)S(1)}, u32[]{:S(2)}, u32[]{:S(2)}) %collective-permute-start.17) | collective-permute-done | bytes 524320 | tf_op jit(solution)/shard_map/ppermute | solution.py:143
  636.9 0.1 constant_dynamic-update-slice_fusion.13
  637.0 0.1 constant_dynamic-update-slice_fusion.12
  637.0 0.1 constant_dynamic-update-slice_fusion.11
  637.1 0.1 constant_dynamic-update-slice_fusion.10
  637.2 0.1 constant_dynamic-update-slice_fusion.9
  637.3 0.1 constant_dynamic-update-slice_fusion.8
  637.4 2.0 copy-done.6
  639.3 14.0 %add_convert_fusion = bf16[1024,4096]{1,0:T(8,128)(2,1)} fusion(bf16[1024,4096]{1,0:T(8,128)(2,1)} %fusion.14, bf16[512,4096]{1,0:T(8,128)(2,1)S(1)} %get-tuple-element.30, bf16[512,4096]{1,0:T(8,128)(2,1)S(1)} %get-tuple-element.29, bf16[1024,2048]{1,0:T(8,128)(2,1)} %copy-done.6, s32[]{:T(128)S(6)} %select_n.96), kind=kOutput, calls=%fused_computation.2 | convolution fusion | flops 8627683328 | bytes 27262980 | tf_op jit(solution)/shard_map/dot_general | solution.py:204
  (47 shorter events, 0.1 us)
Async XLA Ops:
  4.6 94.7 %collective-permute-start.3 = (bf16[2048,1024]{1,0:T(8,128)(2,1)}, bf16[2048,1024]{1,0:T(8,128)(2,1)}, u32[]{:S(2)}, u32[]{:S(2)}) collective-permute-start(bf16[2048,1024]{1,0:T(8,128)(2,1)} %constant_dynamic-slice_fusion.8), channel_id=1, source_target_pairs={{0,2},{2,0},{1,3},{3,1},{4,6},{6,4},{5,7},{7,5},{8,10},{10,8},{9,1... | collective-permute-start | bytes 12582920 | tf_op jit(solution)/shard_map/ppermute | solution.py:152
  7.6 6.2 copy-start
  12.6 175.8 %collective-permute-start.19 = (bf16[512,4096]{1,0:T(8,128)(2,1)}, bf16[512,4096]{1,0:T(8,128)(2,1)}, u32[]{:S(2)}, u32[]{:S(2)}) collective-permute-start(bf16[512,4096]{1,0:T(8,128)(2,1)} %constant_dynamic-slice_fusion), channel_id=1, source_target_pairs={{0,2},{2,0},{1,3},{3,1},{4,6},{6,4},{5,7},{7,5},{8,10},{10,8},{9,1... | collective-permute-start | bytes 12582920 | tf_op jit(solution)/shard_map/ppermute | solution.py:152
  99.3 181.1 %collective-permute-start.4 = (bf16[2048,1024]{1,0:T(8,128)(2,1)}, bf16[2048,1024]{1,0:T(8,128)(2,1)}, u32[]{:S(2)}, u32[]{:S(2)}) collective-permute-start(bf16[2048,1024]{1,0:T(8,128)(2,1)} %collective-permute-done.3), channel_id=1, source_target_pairs={{0,1},{1,0},{2,3},{3,2},{4,5},{5,4},{6,7},{7,6},{8,9},{9,8},{10,11... | collective-permute-start | bytes 12582920 | tf_op jit(solution)/shard_map/ppermute | solution.py:153
  188.3 355.2 %collective-permute-start.20 = (bf16[512,4096]{1,0:T(8,128)(2,1)}, bf16[512,4096]{1,0:T(8,128)(2,1)}, u32[]{:S(2)}, u32[]{:S(2)}) collective-permute-start(bf16[512,4096]{1,0:T(8,128)(2,1)} %collective-permute-done.19), channel_id=1, source_target_pairs={{0,1},{1,0},{2,3},{3,2},{4,5},{5,4},{6,7},{7,6},{8,9},{9,8},{10,11... | collective-permute-start | bytes 12582920 | tf_op jit(solution)/shard_map/ppermute | solution.py:153
  189.6 90.8 %collective-permute-start.10 = (bf16[1024,256]{1,0:T(8,128)(2,1)}, bf16[1024,256]{1,0:T(8,128)(2,1)S(1)}, u32[]{:S(2)}, u32[]{:S(2)}) collective-permute-start(bf16[1024,256]{1,0:T(8,128)(2,1)} %get-tuple-element.41), channel_id=1, source_target_pairs={{0,12},{2,14},{4,0},{6,2},{8,4},{10,6},{12,8},{14,10},{1,13},{3,15... | collective-permute-start | bytes 1572872 | tf_op jit(solution)/shard_map/ppermute | solution.py:143
  193.4 7.7 %copy-start.7 = (s32[1,32,2]{1,2,0:T(2,128)S(1)}, s32[1,32,2]{1,2,0:T(2,128)}, u32[]{:S(2)}) copy-start(s32[1,32,2]{1,2,0:T(2,128)} %param.11) | copy-start | bytes 772
  193.4 7.7 %copy-start.8 = (s32[1,32,2]{1,2,0:T(2,128)S(1)}, s32[1,32,2]{1,2,0:T(2,128)}, u32[]{:S(2)}) copy-start(s32[1,32,2]{1,2,0:T(2,128)} %param.10) | copy-start | bytes 772
  193.4 91.5 %collective-permute-start.8 = (bf16[1024,256]{1,0:T(8,128)(2,1)}, bf16[1024,256]{1,0:T(8,128)(2,1)}, u32[]{:S(2)}, u32[]{:S(2)}) collective-permute-start(bf16[1024,256]{1,0:T(8,128)(2,1)} %get-tuple-element.42), channel_id=1, source_target_pairs={{0,8},{2,10},{4,12},{6,14},{8,0},{10,2},{12,4},{14,6},{1,9},{3,11}... | collective-permute-start | bytes 1572872 | tf_op jit(solution)/shard_map/ppermute | solution.py:143
  200.6 183.4 %collective-permute-start.2 = (bf16[16,2,128,256]{3,2,1,0:T(8,128)(2,1)}, bf16[16,2,128,256]{3,2,1,0:T(8,128)(2,1)S(1)}, u32[]{:S(2)}, u32[]{:S(2)}) collective-permute-start(bf16[16,2,128,256]{3,2,1,0:T(8,128)(2,1)} %get-tuple-element.33), channel_id=1, source_target_pairs={{0,12},{2,14},{4,0},{6,2},{8,4},{10,6},{12,8},{14,10},{1,13},{3,15... | collective-permute-start | bytes 6291464 | tf_op jit(solution)/shard_map/ppermute | solution.py:143
  280.4 4.6 copy-start.4
  280.4 158.1 %collective-permute-start = (bf16[16,2,128,256]{3,2,1,0:T(8,128)(2,1)}, bf16[16,2,128,256]{3,2,1,0:T(8,128)(2,1)S(1)}, u32[]{:S(2)}, u32[]{:S(2)}) collective-permute-start(bf16[16,2,128,256]{3,2,1,0:T(8,128)(2,1)} %get-tuple-element.34), channel_id=1, source_target_pairs={{0,4},{2,6},{4,8},{6,10},{8,12},{10,14},{12,0},{14,2},{1,5},{3,7},... | collective-permute-start | bytes 6291464 | tf_op jit(solution)/shard_map/ppermute | solution.py:143
  280.4 8.5 %slice-start = ((s8[8388608]{0:T(1024)(128)(4,1)}), s8[4194304]{0:T(1024)(128)(4,1)S(1)}, s32[]{:S(2)}) async-start(s8[8388608]{0:T(1024)(128)(4,1)} %bitcast.15), calls=%async_computation | async-start | bytes 8388608
  280.4 4.5 copy-start.5
  280.4 8.5 %slice-start.1 = ((s8[8388608]{0:T(1024)(128)(4,1)}), s8[4194304]{0:T(1024)(128)(4,1)S(1)}, s32[]{:S(2)}) async-start(s8[8388608]{0:T(1024)(128)(4,1)} %bitcast.15), calls=%async_computation.1 | async-start | bytes 8388608
  280.4 160.9 %collective-permute-start.1 = (bf16[16,2,128,256]{3,2,1,0:T(8,128)(2,1)}, bf16[16,2,128,256]{3,2,1,0:T(8,128)(2,1)S(1)}, u32[]{:S(2)}, u32[]{:S(2)}) collective-permute-start(bf16[16,2,128,256]{3,2,1,0:T(8,128)(2,1)} %get-tuple-element.36), channel_id=1, source_target_pairs={{0,8},{2,10},{4,12},{6,14},{8,0},{10,2},{12,4},{14,6},{1,9},{3,11}... | collective-permute-start | bytes 6291464 | tf_op jit(solution)/shard_map/ppermute | solution.py:143
  284.9 98.6 %collective-permute-start.6 = (bf16[1024,256]{1,0:T(8,128)(2,1)S(1)}, bf16[1024,256]{1,0:T(8,128)(2,1)S(1)}, u32[]{:S(2)}, u32[]{:S(2)}) collective-permute-start(bf16[1024,256]{1,0:T(8,128)(2,1)S(1)} %copy-done.5), channel_id=1, source_target_pairs={{0,4},{2,6},{4,8},{6,10},{8,12},{10,14},{12,0},{14,2},{1,5},{3,7},... | collective-permute-start | bytes 1572872 | tf_op jit(solution)/shard_map/ppermute | solution.py:143
  383.6 64.3 %collective-permute-start.11 = (bf16[1024,256]{1,0:T(8,128)(2,1)}, bf16[1024,256]{1,0:T(8,128)(2,1)}, u32[]{:S(2)}, u32[]{:S(2)}) collective-permute-start(bf16[1024,256]{1,0:T(8,128)(2,1)} %get-tuple-element.37), channel_id=1, source_target_pairs={{0,14},{2,12},{4,2},{6,0},{8,6},{10,4},{12,10},{14,8},{1,15},{3,13... | collective-permute-start | bytes 1572872 | tf_op jit(solution)/shard_map/ppermute | solution.py:143
  384.0 57.4 %copy-start.1 = (bf16[16,2,128,256]{3,2,1,0:T(8,128)(2,1)}, bf16[16,2,128,256]{3,2,1,0:T(8,128)(2,1)S(1)}, u32[]{:S(2)}) copy-start(bf16[16,2,128,256]{3,2,1,0:T(8,128)(2,1)S(1)} %collective-permute-done.2.refs_3_) | copy-start | bytes 6291460
  384.0 81.1 %collective-permute-start.9 = (bf16[1024,256]{1,0:T(8,128)(2,1)}, bf16[1024,256]{1,0:T(8,128)(2,1)}, u32[]{:S(2)}, u32[]{:S(2)}) collective-permute-start(bf16[1024,256]{1,0:T(8,128)(2,1)} %get-tuple-element.38), channel_id=1, source_target_pairs={{0,10},{2,8},{4,14},{6,12},{8,2},{10,0},{12,6},{14,4},{1,11},{3,9}... | collective-permute-start | bytes 1572872 | tf_op jit(solution)/shard_map/ppermute | solution.py:143
  438.5 2.9 copy-start.2
  438.5 44.3 %collective-permute-start.7 = (bf16[1024,256]{1,0:T(8,128)(2,1)}, bf16[1024,256]{1,0:T(8,128)(2,1)}, u32[]{:S(2)}, u32[]{:S(2)}) collective-permute-start(bf16[1024,256]{1,0:T(8,128)(2,1)} %get-tuple-element.39), channel_id=1, source_target_pairs={{0,6},{2,4},{4,10},{6,8},{8,14},{10,12},{12,2},{14,0},{1,7},{3,5},... | collective-permute-start | bytes 1572872 | tf_op jit(solution)/shard_map/ppermute | solution.py:143
  441.3 1.3 copy-start.3
  441.3 41.4 %collective-permute-start.5 = (bf16[1024,256]{1,0:T(8,128)(2,1)}, bf16[1024,256]{1,0:T(8,128)(2,1)S(1)}, u32[]{:S(2)}, u32[]{:S(2)}) collective-permute-start(bf16[1024,256]{1,0:T(8,128)(2,1)} %get-tuple-element.40), channel_id=1, source_target_pairs={{0,2},{2,0},{4,6},{6,4},{8,10},{10,8},{12,14},{14,12},{1,3},{3,1},... | collective-permute-start | bytes 1572872 | tf_op jit(solution)/shard_map/ppermute | solution.py:143
  541.3 12.5 %collective-permute-start.12 = (bf16[1024,256]{1,0:T(8,128)(2,1)S(1)}, bf16[1024,256]{1,0:T(8,128)(2,1)S(1)}, u32[]{:S(2)}, u32[]{:S(2)}) collective-permute-start(bf16[1024,256]{1,0:T(8,128)(2,1)S(1)} %get-tuple-element.14), channel_id=1, source_target_pairs={{0,12},{2,14},{4,0},{6,2},{8,4},{10,6},{12,8},{14,10},{1,13},{3,15... | collective-permute-start | bytes 1572872 | tf_op jit(solution)/shard_map/ppermute | solution.py:143
  541.4 46.9 %collective-permute-start.13 = (bf16[1024,256]{1,0:T(8,128)(2,1)S(1)}, bf16[1024,256]{1,0:T(8,128)(2,1)S(1)}, u32[]{:S(2)}, u32[]{:S(2)}) collective-permute-start(bf16[1024,256]{1,0:T(8,128)(2,1)S(1)} %get-tuple-element.15), channel_id=1, source_target_pairs={{0,8},{2,10},{4,12},{6,14},{8,0},{10,2},{12,4},{14,6},{1,9},{3,11}... | collective-permute-start | bytes 1572872 | tf_op jit(solution)/shard_map/ppermute | solution.py:143
  541.8 51.7 %slice-start.2 = ((s8[8388608]{0:T(1024)(128)(4,1)}), s8[4194304]{0:T(1024)(128)(4,1)S(1)}, s32[]{:S(2)}) async-start(s8[8388608]{0:T(1024)(128)(4,1)} %bitcast.17), calls=%async_computation.2 | async-start | bytes 8388608
  541.8 51.7 %slice-start.3 = ((s8[8388608]{0:T(1024)(128)(4,1)}), s8[4194304]{0:T(1024)(128)(4,1)S(1)}, s32[]{:S(2)}) async-start(s8[8388608]{0:T(1024)(128)(4,1)} %bitcast.17), calls=%async_computation.3 | async-start | bytes 8388608
  541.8 47.3 %collective-permute-start.14 = (bf16[1024,256]{1,0:T(8,128)(2,1)S(1)}, bf16[1024,256]{1,0:T(8,128)(2,1)S(1)}, u32[]{:S(2)}, u32[]{:S(2)}) collective-permute-start(bf16[1024,256]{1,0:T(8,128)(2,1)S(1)} %get-tuple-element.16), channel_id=1, source_target_pairs={{0,4},{2,6},{4,8},{6,10},{8,12},{10,14},{12,0},{14,2},{1,5},{3,7},... | collective-permute-start | bytes 1572872 | tf_op jit(solution)/shard_map/ppermute | solution.py:143
  548.0 58.1 %collective-permute-start.15 = (bf16[1024,256]{1,0:T(8,128)(2,1)S(1)}, bf16[1024,256]{1,0:T(8,128)(2,1)S(1)}, u32[]{:S(2)}, u32[]{:S(2)}) collective-permute-start(bf16[1024,256]{1,0:T(8,128)(2,1)S(1)} %get-tuple-element.17), channel_id=1, source_target_pairs={{0,2},{2,0},{4,6},{6,4},{8,10},{10,8},{12,14},{14,12},{1,3},{3,1},... | collective-permute-start | bytes 1572872 | tf_op jit(solution)/shard_map/ppermute | solution.py:143
  549.6 56.5 %collective-permute-start.16 = (bf16[1024,256]{1,0:T(8,128)(2,1)S(1)}, bf16[1024,256]{1,0:T(8,128)(2,1)S(1)}, u32[]{:S(2)}, u32[]{:S(2)}) collective-permute-start(bf16[1024,256]{1,0:T(8,128)(2,1)S(1)} %get-tuple-element.18), channel_id=1, source_target_pairs={{0,14},{2,12},{4,2},{6,0},{8,6},{10,4},{12,10},{14,8},{1,15},{3,13... | collective-permute-start | bytes 1572872 | tf_op jit(solution)/shard_map/ppermute | solution.py:143
  553.8 83.1 %collective-permute-start.17 = (bf16[1024,256]{1,0:T(8,128)(2,1)S(1)}, bf16[1024,256]{1,0:T(8,128)(2,1)S(1)}, u32[]{:S(2)}, u32[]{:S(2)}) collective-permute-start(bf16[1024,256]{1,0:T(8,128)(2,1)S(1)} %get-tuple-element.19), channel_id=1, source_target_pairs={{0,10},{2,8},{4,14},{6,12},{8,2},{10,0},{12,6},{14,4},{1,11},{3,9}... | collective-permute-start | bytes 1572872 | tf_op jit(solution)/shard_map/ppermute | solution.py:143
  588.3 48.7 %collective-permute-start.18 = (bf16[1024,256]{1,0:T(8,128)(2,1)S(1)}, bf16[1024,256]{1,0:T(8,128)(2,1)S(1)}, u32[]{:S(2)}, u32[]{:S(2)}) collective-permute-start(bf16[1024,256]{1,0:T(8,128)(2,1)S(1)} %get-tuple-element.20), channel_id=1, source_target_pairs={{0,6},{2,4},{4,10},{6,8},{8,14},{10,12},{12,2},{14,0},{1,7},{3,5},... | collective-permute-start | bytes 1572872 | tf_op jit(solution)/shard_map/ppermute | solution.py:143
  637.3 2.0 copy-start.6

commit v2 on v0

v2 whole, which is shorter than its diff:
```python
import functools

import jax
import jax.numpy as jnp
from jax import lax
from jax.experimental import pallas as pl
from jax.experimental.pallas import tpu as pltpu
from jax.sharding import PartitionSpec as P

DH = 128
BLOCK = 64
KN = 2


def plain_body(tokens, w_query, w_out, neighbour_kv, shard_lists, slot_lists):
    local_seqs, local_span, feature_count = tokens.shape
    local_heads = w_query.shape[1] // DH
    widened = tokens.astype(jnp.float32)
    normed = (
        widened * lax.rsqrt(jnp.mean(widened * widened, axis=2, keepdims=True) + 1e-06)
    ).astype(jnp.bfloat16)
    product = jnp.einsum(
        "std,dh->sth",
        lax.all_gather(normed, "head", axis=0, tiled=True),
        w_query,
        preferred_element_type=jnp.float32,
    )
    queries = (product * DH ** (-0.5)).astype(jnp.bfloat16)
    seq_rep = queries.shape[0]
    own_blocks = seq_rep * local_span // BLOCK
    queries = queries.reshape(own_blocks, BLOCK, local_heads, DH)
    store_count = neighbour_kv.shape[0]
    row_shape = neighbour_kv.shape[1:]
    wanted = shard_lists[0] * store_count + slot_lists[0]
    pieces = lax.all_gather(neighbour_kv, "seq", axis=0, tiled=True)
    fetched = jnp.take(pieces, wanted.reshape(-1), axis=0).reshape((own_blocks, KN) + row_shape)
    key_rows = fetched[:, :, 0].reshape(own_blocks, KN * row_shape[1], local_heads, DH)
    value_rows = fetched[:, :, 1].reshape(own_blocks, KN * row_shape[1], local_heads, DH)
    scores = jnp.einsum("oqhd,okhd->ohqk", queries, key_rows, preferred_element_type=jnp.float32)
    weights = jax.nn.softmax(scores, axis=-1).astype(jnp.bfloat16)
    context = jnp.einsum(
        "ohqk,okhd->oqhd", weights, value_rows, preferred_element_type=jnp.float32
    ).astype(jnp.bfloat16)
    context = context.reshape(seq_rep, local_span, local_heads * DH)
    return lax.psum_scatter(
        jnp.einsum("sth,hd->std", context, w_out, preferred_element_type=jnp.float32).astype(
            jnp.bfloat16
        ),
        "head",
        scatter_dimension=0,
        tiled=True,
    )


MESH = pl.DeviceIdType.MESH
ROW_TILE = 512
NORM_TILE = 32


def flow_kernel(
    n_seq, n_head, tokens, w_query, w_out, kv, lists,
    context, w_out_other,
    store, q_in, q_out, c_out, normed, wq_own, wq_other, lists_in, picks,
    kv_send, kv_recv, q_send, q_recv, c_send, c_recv, w_send, w_recv, l_send, l_recv, local, token_sem,
):
    s = lax.axis_index("seq")
    x = lax.axis_index("head")
    r = lax.axis_index("rep")
    rows, features = tokens.shape
    count = kv.shape[0]
    width = q_in.shape[2]
    heads = width // DH
    blocks = rows // BLOCK
    pieces = n_seq * n_head

    def peer(dz, dx):
        return {
            "seq": lax.rem(s + dz + n_seq, n_seq),
            "head": lax.rem(x + dx + n_head, n_head),
        }

    def cols(index):
        return pl.ds(pl.multiple_of(index * width, width), width)

    def remote(src, dst, send, recv, device):
        return pltpu.make_async_remote_copy(
            src_ref=src, dst_ref=dst, send_sem=send, recv_sem=recv, device_id=device, device_id_type=MESH
        )

    barrier = pltpu.get_barrier_semaphore()
    for p in range(1, pieces):
        pl.semaphore_signal(barrier, inc=1, device_id=peer(p // n_head, p % n_head), device_id_type=MESH)
    pl.semaphore_signal(barrier, inc=1, device_id={"rep": 1 - r}, device_id_type=MESH)
    pl.semaphore_wait(barrier, pieces)

    def kv_copy(dz):
        to = lax.rem(s + dz, n_seq)
        return remote(
            kv.at[:, :, :, cols(to)], store.at[pl.ds(s * count, count)],
            kv_send.at[dz], kv_recv.at[dz], peer(dz, 0),
        )

    def list_copy(dz):
        return remote(lists, lists_in.at[dz], l_send.at[dz], l_recv.at[dz], peer(dz, 0))

    def q_copy(p):
        return remote(
            q_out.at[p], q_in.at[p], q_send.at[p], q_recv.at[p], peer(p // n_head, p % n_head)
        )

    def c_copy(p):
        dz, dx = p // n_head, p % n_head
        return remote(
            c_out.at[p], context.at[dx, :, cols(s)], c_send.at[p], c_recv.at[p], peer(-dz, -dx)
        )

    half = features // 2
    wq_rows = pl.ds(pl.multiple_of(r * half, half), half)
    wq_x = remote(w_query.at[wq_rows], wq_other.at[wq_rows], w_send.at[0], w_recv.at[0], peer(0, 1))
    wq_c = remote(
        wq_other.at[wq_rows], wq_other.at[wq_rows], w_send.at[1], w_recv.at[1], {"rep": 1 - r}
    )
    wo_half = w_out.shape[0] // 2
    wo_rows = pl.ds(pl.multiple_of(r * wo_half, wo_half), wo_half)
    wo_x = remote(w_out.at[wo_rows], w_out_other.at[wo_rows], w_send.at[2], w_recv.at[2], peer(0, 1))
    wo_c = remote(
        w_out_other.at[wo_rows], w_out_other.at[wo_rows], w_send.at[3], w_recv.at[3], {"rep": 1 - r}
    )

    tiles = 4
    tile_rows = rows // tiles
    token_copies = [
        pltpu.make_async_copy(
            tokens.at[pl.ds(t * tile_rows, tile_rows)], normed.at[pl.ds(t * tile_rows, tile_rows)],
            token_sem.at[t],
        )
        for t in range(tiles)
    ]
    wq_local = pltpu.make_async_copy(w_query, wq_own, local.at[0])
    kv_local = pltpu.make_async_copy(
        kv.at[:, :, :, cols(s)], store.at[pl.ds(s * count, count)], local.at[1]
    )
    list_local = pltpu.make_async_copy(lists, lists_in.at[0], local.at[2])

    wq_x.start()
    for copy in token_copies:
        copy.start()
    for dz in range(1, n_seq):
        list_copy(dz).start()
    for dz in range(1, n_seq):
        kv_copy(dz).start()
    wq_local.start()
    list_local.start()
    kv_local.start()

    def norm(t, carry):
        span = pl.ds(pl.multiple_of(t * NORM_TILE, NORM_TILE), NORM_TILE)
        wide = normed[span, :].astype(jnp.float32)
        scale = lax.rsqrt(jnp.mean(wide * wide, axis=1, keepdims=True) + 1e-06)
        normed[span, :] = (wide * scale).astype(jnp.bfloat16)
        return carry

    per_tile = tile_rows // NORM_TILE
    for t in range(tiles):
        token_copies[t].wait()
        lax.fori_loop(t * per_tile, (t + 1) * per_tile, norm, 0)

    def project(w, to, dst):
        def tile(t, carry):
            span = pl.ds(pl.multiple_of(t * ROW_TILE, ROW_TILE), ROW_TILE)
            product = jnp.dot(normed[span, :], w[:, cols(to)], preferred_element_type=jnp.float32)
            dst[span, :] = (product * DH ** (-0.5)).astype(jnp.bfloat16)
            return carry

        lax.fori_loop(0, rows // ROW_TILE, tile, 0)

    def project_send(w, dx, first):
        def one(dz, carry):
            p = dz * n_head + dx
            project(w, lax.rem(s + dz, n_seq), q_out.at[p])
            q_copy(p).start()
            return carry

        lax.fori_loop(first, n_seq, one, 0)

    wq_local.wait()
    project_send(wq_own, 0, 1)
    wq_x.wait_recv()
    wq_c.start()
    project(wq_own, s, q_in.at[0])
    wq_c.wait_recv()
    project_send(wq_other, 1, 0)
    wo_x.start()

    list_local.wait()
    for dz in range(1, n_seq):
        list_copy(dz).wait_recv()
    picks_copy = pltpu.make_async_copy(lists_in, picks, local.at[3])
    picks_copy.start()
    picks_copy.wait()
    kv_local.wait()
    for dz in range(1, n_seq):
        kv_copy(dz).wait_recv()
    wo_x.wait_recv()
    wo_c.start()

    blank = jnp.zeros((BLOCK, DH), jnp.bfloat16)

    def attend(p):
        dz, dx = p // n_head, p % n_head
        base = lax.rem(x - dx + n_head, n_head) * blocks

        def step(block, carry):
            at = (base + block) * KN
            chosen = [picks[dz, 0, at + k] for k in range(KN)]
            keys = jnp.concatenate([store[i, 0] for i in chosen], axis=0)
            values = jnp.concatenate([store[i, 1] for i in chosen], axis=0)
            span = pl.ds(pl.multiple_of(block * BLOCK, BLOCK), BLOCK)
            q = q_in[p, span, :]
            spread = jnp.concatenate(
                [
                    jnp.concatenate(
                        [q[:, h * DH:(h + 1) * DH] if h == g else blank for h in range(heads)], axis=1
                    )
                    for g in range(heads)
                ],
                axis=0,
            )
            scores = lax.dot_general(
                spread, keys, (((1,), (1,)), ((), ())), preferred_element_type=jnp.float32
            )
            grown = jnp.exp(scores - jnp.max(scores, axis=-1, keepdims=True))
            weights = (grown / jnp.sum(grown, axis=-1, keepdims=True)).astype(jnp.bfloat16)
            mixed = jnp.dot(weights, values, preferred_element_type=jnp.float32)
            c_out[p, span, :] = jnp.concatenate(
                [mixed[h * BLOCK:(h + 1) * BLOCK, h * DH:(h + 1) * DH] for h in range(heads)], axis=1
            ).astype(jnp.bfloat16)
            return carry

        lax.fori_loop(0, blocks, step, 0, unroll=4 if blocks % 4 == 0 else 1)

    def remote_piece(t, carry):
        p = lax.rem(t // n_head + 1, n_seq) * n_head + (n_head - 1 - lax.rem(t, n_head))
        q_copy(p).wait_recv()
        attend(p)
        c_copy(p).start()
        return carry

    lax.fori_loop(0, pieces - 1, remote_piece, 0)
    attend(0)
    own = pltpu.make_async_copy(c_out.at[0], context.at[0, :, cols(s)], local.at[4])
    own.start()

    for dz in range(1, n_seq):
        kv_copy(dz).wait_send()
        list_copy(dz).wait_send()
    for copy in (wq_x, wq_c, wo_x, wo_c):
        copy.wait_send()
    wo_c.wait_recv()
    for p in range(1, pieces):
        q_copy(p).wait_send()
    for p in range(1, pieces):
        c_copy(p).wait_send()
        c_copy(p).wait_recv()
    own.wait()


def spread_body(n_seq, n_head, tokens, w_query, w_out, neighbour_kv, shard_lists, slot_lists):
    local_seqs, local_span, features = tokens.shape
    rows = local_seqs * local_span
    local_width = w_query.shape[1]
    width = local_width // n_seq
    count, _, length, _ = neighbour_kv.shape
    pieces = n_seq * n_head
    places = (shard_lists[0] * count + slot_lists[0]).reshape(1, -1).astype(jnp.int32)
    lanes = -(-places.shape[1] // 128) * 128
    places = jnp.pad(places, ((0, 7), (0, lanes - places.shape[1])))
    bf16 = jnp.bfloat16
    anywhere = pl.BlockSpec(memory_space=pl.ANY)
    dma = pltpu.SemaphoreType.DMA
    context, w_out_other = pl.pallas_call(
        functools.partial(flow_kernel, n_seq, n_head),
        out_shape=[
            jax.ShapeDtypeStruct((n_head, rows, local_width), bf16),
            jax.ShapeDtypeStruct(w_out.shape, bf16),
        ],
        in_specs=[anywhere] * 4 + [pl.BlockSpec(memory_space=pltpu.VMEM)],
        out_specs=[anywhere] * 2,
        scratch_shapes=[
            pltpu.VMEM((n_seq * count, 2, length, width), bf16),
            pltpu.VMEM((pieces, rows, width), bf16),
            pltpu.VMEM((pieces, rows, width), bf16),
            pltpu.VMEM((pieces, rows, width), bf16),
            pltpu.VMEM((rows, features), bf16),
            pltpu.VMEM((features, local_width), bf16),
            pltpu.VMEM((features, local_width), bf16),
            pltpu.VMEM((n_seq, 8, lanes), jnp.int32),
            pltpu.SMEM((n_seq, 8, lanes), jnp.int32),
            dma((n_seq,)), dma((n_seq,)),
            dma((pieces,)), dma((pieces,)),
            dma((pieces,)), dma((pieces,)),
            dma((4,)), dma((4,)),
            dma((n_seq,)), dma((n_seq,)),
            dma((5,)), dma((4,)),
        ],
        compiler_params=pltpu.CompilerParams(
            collective_id=0, has_side_effects=True, vmem_limit_bytes=58 * 2**20
        ),
        cost_estimate=pl.CostEstimate(
            flops=2 * rows * features * local_width * n_head, bytes_accessed=2**26, transcendentals=2**22
        ),
        name="flow",
    )(tokens.reshape(rows, features), w_query, w_out, neighbour_kv, places)
    terms = [
        lax.reduce_precision(
            jnp.dot(context[dx], w, preferred_element_type=jnp.float32), exponent_bits=8, mantissa_bits=7
        )
        for dx, w in enumerate([w_out, w_out_other])
    ]
    return (terms[0] + terms[1]).astype(bf16).reshape(local_seqs, local_span, w_out.shape[1])


def solution(mesh):
    placed = (
        P(("grp", "rep", "head"), "seq", None),
        P(None, "head"),
        P("head", None),
        P(("grp", "seq", "rep"), None, None, "head"),
        P(("grp", "seq", "rep"), None, None),
        P(("grp", "seq", "rep"), None, None),
    )
    sizes = dict(mesh.shape)
    n_seq, n_head = sizes["seq"], sizes["head"]

    def body(*arrays):
        local_heads = arrays[1].shape[1] // DH
        if n_head == 2 and sizes["rep"] == 2 and local_heads % n_seq == 0:
            return spread_body(n_seq, n_head, *arrays)
        return plain_body(*arrays)

    return jax.shard_map(
        body,
        mesh=mesh,
        in_specs=placed,
        out_specs=P(("grp", "rep", "head"), "seq", None),
        check_vma=False,
    )
```

time: 1140 us -> 443 us (0.39)
  waiting for transfers between devices: 928 us -> 0 us
  Pallas kernels: 0 us -> 410 us
  local copies, waits for them, and re-layouts: 76.7 us -> 0.8 us
  matrix products: 80.4 us -> 31.3 us
  other arithmetic: 38.2 us -> 0.7 us
  between operations: 13.2 us -> 0.02 us
    all_gather x2 -> x0, waiting for transfers between devices: 737 us -> none  [the longest x1 537 us: body(): pieces = lax.all_gather(neighbour_kv, 'seq', axis=0, tiled=True)]
    pallas_call x0 -> x1, Pallas kernels: none -> 410 us  [spread_body(): pl.pallas_call(functools.partial(flow_kernel, n_seq, n_head), out_shape=[...]
    reduce_scatter x1 -> x0, waiting for transfers between devices: 189 us -> none  [body(): lax.psum_scatter(jnp.einsum('sth,hd->std', context, w_out, preferred_elem...]
    dot_general x3 -> x2, matrix products: 62.9 us -> 31.3 us  [spread_body(): jnp.dot(context[dx], w, preferred_element_type=jnp.float32)]
    select_n x2 -> x0, other arithmetic: 22.9 us -> none  [the longest x1 22.9 us: body(): fetched = jnp.where(inside[:, :, None, None, None], picked_rows, blank_rows)]
    gather x1 -> x0, local copies, waits for them, and re-layouts: 22.7 us -> none  [body(): picked_rows = jnp.take(pieces, clipped, axis=0).reshape(blank_rows.shape)]
    unnamed x7 -> x2, local copies, waits for them, and re-layouts: 21.3 us -> 0.01 us
    sub x1 -> x0, matrix products: 17.5 us -> none  [body(): weights = jax.nn.softmax(scores, axis=-1).astype(jnp.bfloat16)]
  transfers between devices with their start and end apart: 3 -> 0, of which waited for: 3 -> 0; matrix products, arithmetic and copies ran while one was open for 2% -> 0% of each run, Pallas kernels for 0% -> 0%
where the time goes in v2:
time: 443 us
  Pallas kernels  410 us (93%)
  matrix products  31.3 us (7%)
    pallas_call x1, Pallas kernels, spread_body(): pl.pallas_call(functools.partial(flow_kernel, n_seq, n_head), out_shape=[...  410 us
    dot_general x2, matrix products, spread_body(): jnp.dot(context[dx], w, preferred_element_type=jnp.float32)  31.3 us

profile of v2, /device:TPU:0, one launch (start us, length us, event | category | flops | bytes accessed | tf_op | source)
XLA Modules:
  0.0 443.0 jit_solution(2648800434446992163)
XLA Ops:
  0.0 0.7 multiply_add_fusion
  0.7 0.1 copy.8
  0.8 0.1 add.19
  0.9 0.6 pad.4.lists
  1.5 410.2 %flow.1 = (bf16[2,1024,1024]{2,1,0:T(8,128)(2,1)}, bf16[1024,4096]{1,0:T(8,128)(2,1)}) custom-call(bf16[1024,4096]{1,0:T(8,128)(2,1)} %bitcast.10, bf16[4096,1024]{1,0:T(8,128)(2,1)} %w_query.1, bf16[1024,4096]{1,0:T(8,128)(2,1)} %w_out.1, bf16[16,2,128,1024]{3,2,1,0:T(8,128)(2,1)} %kv.1, s32[8,128]{1,0:T(8,128)} %pad.4.lists), custom_call_target="tpu_custom_call" | custom-call | flops 17179869184 | bytes 67108864 | tf_op jit(solution)/shard_map/flow/pallas_call | solution.py:281
  411.8 0.0 copy-start
  411.8 16.1 %fusion.1 = f32[1024,4096]{1,0:T(8,128)} fusion(bf16[1024,4096]{1,0:T(8,128)(2,1)} %w_out.1, bf16[2,1024,1024]{2,1,0:T(8,128)(2,1)} %get-tuple-element.7), kind=kOutput, calls=%fused_computation.2 | convolution fusion | flops 8589934592 | bytes 27262976 | tf_op jit(solution)/shard_map/dot_general | solution.py:316
  427.9 0.0 copy-done
  427.9 15.2 %add_convert_fusion = bf16[1024,4096]{1,0:T(8,128)(2,1)} fusion(f32[1024,4096]{1,0:T(8,128)} %fusion.1, bf16[1024,4096]{1,0:T(8,128)(2,1)S(1)} %copy-done, bf16[2,1024,1024]{2,1,0:T(8,128)(2,1)} %get-tuple-element.7), kind=kOutput, calls=%fused_computation | convolution fusion | flops 8606711808 | bytes 35651584 | tf_op jit(solution)/shard_map/dot_general | solution.py:316
Async XLA Ops:
  411.8 16.1 %copy-start = (bf16[1024,4096]{1,0:T(8,128)(2,1)S(1)}, bf16[1024,4096]{1,0:T(8,128)(2,1)}, u32[]{:S(2)}) copy-start(bf16[1024,4096]{1,0:T(8,128)(2,1)} %get-tuple-element.8) | copy-start | bytes 25165828

commit v3 on v2

--- a/solution.py
+++ b/solution.py
@@ -54,14 +54,17 @@
 
 MESH = pl.DeviceIdType.MESH
 ROW_TILE = 512
+CHUNKS = 4
+LAG = 2
 NORM_TILE = 32
 
 
 def flow_kernel(
     n_seq, n_head, tokens, w_query, w_out, kv, lists,
-    context, w_out_other,
-    store, q_in, q_out, c_out, normed, wq_own, wq_other, lists_in, picks,
+    crossed, w_out_other,
+    context, store, q_in, q_out, c_out, normed, wq_own, wq_other, lists_in, picks,
     kv_send, kv_recv, q_send, q_recv, c_send, c_recv, w_send, w_recv, l_send, l_recv, local, token_sem,
+    own_sem, out_sem, load_sem,
 ):
     s = lax.axis_index("seq")
     x = lax.axis_index("head")
@@ -103,16 +106,53 @@
     def list_copy(dz):
         return remote(lists, lists_in.at[dz], l_send.at[dz], l_recv.at[dz], peer(dz, 0))
 
-    def q_copy(p):
+    chunk_rows = rows // CHUNKS
+    chunk_blocks = blocks // CHUNKS
+
+    def chunk_span(c):
+        return pl.ds(pl.multiple_of(c * chunk_rows, chunk_rows), chunk_rows)
+
+    def q_copy(p, c):
+        span = chunk_span(c)
         return remote(
-            q_out.at[p], q_in.at[p], q_send.at[p], q_recv.at[p], peer(p // n_head, p % n_head)
-        )
-
-    def c_copy(p):
+            q_out.at[p, span], q_in.at[p, span], q_send.at[p, c], q_recv.at[p, c],
+            peer(p // n_head, p % n_head),
+        )
+
+    def c_copy(p, c):
         dz, dx = p // n_head, p % n_head
+        span = chunk_span(c)
         return remote(
-            c_out.at[p], context.at[dx, :, cols(s)], c_send.at[p], c_recv.at[p], peer(-dz, -dx)
-        )
+            c_out.at[p, span], context.at[dx, span, cols(s)], c_send.at[p, c], c_recv.at[p, c],
+            peer(-dz, -dx),
+        )
+
+    def own_copy(c):
+        span = chunk_span(c)
+        return pltpu.make_async_copy(
+            c_out.at[0, span], context.at[0, span, cols(s)], own_sem.at[c]
+        )
+
+    def out_copy(c):
+        span = chunk_span(c)
+        return pltpu.make_async_copy(normed.at[span], crossed.at[span], out_sem.at[c])
+
+    local_width = w_out.shape[0]
+    out_tiles = features // local_width
+
+    def w_load(source, target, which, t):
+        return pltpu.make_async_copy(
+            source.at[:, pl.ds(t * local_width, local_width)],
+            target.at[pl.ds(t * local_width, local_width)],
+            load_sem.at[which, t],
+        )
+
+    def far_piece(u):
+        dz = lax.rem(u // n_head + n_seq // 2 - 1, n_seq - 1) + 1
+        return dz * n_head + (n_head - 1 - lax.rem(u, n_head))
+
+    far = (n_seq - 1) * n_head
+    far_order = [(t + n_seq // 2 - 1) % (n_seq - 1) + 1 for t in range(n_seq - 1)]
 
     half = features // 2
     wq_rows = pl.ds(pl.multiple_of(r * half, half), half)
@@ -147,7 +187,7 @@
         copy.start()
     for dz in range(1, n_seq):
         list_copy(dz).start()
-    for dz in range(1, n_seq):
+    for dz in far_order:
         kv_copy(dz).start()
     wq_local.start()
     list_local.start()
@@ -174,23 +214,33 @@
 
         lax.fori_loop(0, rows // ROW_TILE, tile, 0)
 
-    def project_send(w, dx, first):
+    def project_all(w, dx, first):
         def one(dz, carry):
-            p = dz * n_head + dx
-            project(w, lax.rem(s + dz, n_seq), q_out.at[p])
-            q_copy(p).start()
+            project(w, lax.rem(s + dz, n_seq), q_out.at[dz * n_head + dx])
             return carry
 
         lax.fori_loop(first, n_seq, one, 0)
 
     wq_local.wait()
-    project_send(wq_own, 0, 1)
+    project(wq_own, s, q_in.at[0])
+    project_all(wq_own, 0, 1)
+    for t in range(out_tiles):
+        w_load(w_out, wq_own, 0, t).start()
     wq_x.wait_recv()
+    wo_x.start()
     wq_c.start()
-    project(wq_own, s, q_in.at[0])
     wq_c.wait_recv()
-    project_send(wq_other, 1, 0)
-    wo_x.start()
+    project_all(wq_other, 1, 0)
+    for c in range(CHUNKS):
+        q_copy(1, c).start()
+    for dz in range(1, n_seq):
+        kv_copy(dz).wait_send()
+
+    def q_start(t, carry):
+        q_copy(far_piece(lax.rem(t, far)), t // far).start()
+        return carry
+
+    lax.fori_loop(0, far * CHUNKS, q_start, 0)
 
     list_local.wait()
     for dz in range(1, n_seq):
@@ -203,14 +253,17 @@
         kv_copy(dz).wait_recv()
     wo_x.wait_recv()
     wo_c.start()
+    wq_x.wait_send()
+    wq_c.wait_send()
 
     blank = jnp.zeros((BLOCK, DH), jnp.bfloat16)
 
-    def attend(p):
+    def attend(p, c):
         dz, dx = p // n_head, p % n_head
         base = lax.rem(x - dx + n_head, n_head) * blocks
 
         def step(block, carry):
+            block = c * chunk_blocks + block
             at = (base + block) * KN
             chosen = [picks[dz, 0, at + k] for k in range(KN)]
             keys = jnp.concatenate([store[i, 0] for i in chosen], axis=0)
@@ -237,32 +290,72 @@
             ).astype(jnp.bfloat16)
             return carry
 
-        lax.fori_loop(0, blocks, step, 0, unroll=4 if blocks % 4 == 0 else 1)
-
-    def remote_piece(t, carry):
-        p = lax.rem(t // n_head + 1, n_seq) * n_head + (n_head - 1 - lax.rem(t, n_head))
-        q_copy(p).wait_recv()
-        attend(p)
-        c_copy(p).start()
+        lax.fori_loop(0, chunk_blocks, step, 0, unroll=4 if chunk_blocks % 4 == 0 else 1)
+
+    def output(c):
+        span = chunk_span(c)
+        own_copy(c).wait()
+        for p in range(1, pieces):
+            c_copy(p, c).wait_recv()
+
+        def tile(t, carry):
+            depth = pl.ds(pl.multiple_of(t * local_width, local_width), local_width)
+            total = jnp.zeros((chunk_rows, local_width), jnp.float32)
+            for dx, w in enumerate((wq_own, wq_other)):
+                term = jnp.dot(context[dx, span, :], w[depth, :], preferred_element_type=jnp.float32)
+                total = total + term.astype(jnp.bfloat16).astype(jnp.float32)
+            normed[span, depth] = total.astype(jnp.bfloat16)
+            return carry
+
+        lax.fori_loop(0, out_tiles, tile, 0)
+        out_copy(c).start()
+
+    def turn(c, carry):
+        @pl.when(c < CHUNKS)
+        def _():
+            attend(0, c)
+            own_copy(c).start()
+
+            def one(t, carry):
+                p = jnp.where(t == 0, 1, far_piece(jnp.maximum(t - 1, 0)))
+                q_copy(p, c).wait_recv()
+                attend(p, c)
+                c_copy(p, c).start()
+                return carry
+
+            lax.fori_loop(0, pieces - 1, one, 0)
+
+        @pl.when(c == LAG)
+        def _():
+            wo_c.wait_recv()
+            for t in range(out_tiles):
+                w_load(w_out_other, wq_other, 1, t).start()
+            for t in range(out_tiles):
+                w_load(w_out, wq_own, 0, t).wait()
+                w_load(w_out_other, wq_other, 1, t).wait()
+
+        @pl.when(c >= LAG)
+        def _():
+            output(c - LAG)
+
         return carry
 
-    lax.fori_loop(0, pieces - 1, remote_piece, 0)
-    attend(0)
-    own = pltpu.make_async_copy(c_out.at[0], context.at[0, :, cols(s)], local.at[4])
-    own.start()
+    lax.fori_loop(0, CHUNKS + LAG, turn, 0)
 
     for dz in range(1, n_seq):
-        kv_copy(dz).wait_send()
         list_copy(dz).wait_send()
-    for copy in (wq_x, wq_c, wo_x, wo_c):
+    for copy in (wo_x, wo_c):
         copy.wait_send()
-    wo_c.wait_recv()
-    for p in range(1, pieces):
-        q_copy(p).wait_send()
-    for p in range(1, pieces):
-        c_copy(p).wait_send()
-        c_copy(p).wait_recv()
-    own.wait()
+
+    def drain(t, carry):
+        p, c = t // CHUNKS + 1, lax.rem(t, CHUNKS)
+        q_copy(p, c).wait_send()
+        c_copy(p, c).wait_send()
+        return carry
+
+    lax.fori_loop(0, (pieces - 1) * CHUNKS, drain, 0)
+    for c in range(CHUNKS):
+        out_copy(c).wait()
 
 
 def spread_body(n_seq, n_head, tokens, w_query, w_out, neighbour_kv, shard_lists, slot_lists):
@@ -278,15 +371,16 @@
     bf16 = jnp.bfloat16
     anywhere = pl.BlockSpec(memory_space=pl.ANY)
     dma = pltpu.SemaphoreType.DMA
-    context, w_out_other = pl.pallas_call(
+    crossed, _ = pl.pallas_call(
         functools.partial(flow_kernel, n_seq, n_head),
         out_shape=[
-            jax.ShapeDtypeStruct((n_head, rows, local_width), bf16),
+            jax.ShapeDtypeStruct((rows, w_out.shape[1]), bf16),
             jax.ShapeDtypeStruct(w_out.shape, bf16),
         ],
         in_specs=[anywhere] * 4 + [pl.BlockSpec(memory_space=pltpu.VMEM)],
         out_specs=[anywhere] * 2,
         scratch_shapes=[
+            pltpu.VMEM((n_head, rows, local_width), bf16),
             pltpu.VMEM((n_seq * count, 2, length, width), bf16),
             pltpu.VMEM((pieces, rows, width), bf16),
             pltpu.VMEM((pieces, rows, width), bf16),
@@ -297,11 +391,12 @@
             pltpu.VMEM((n_seq, 8, lanes), jnp.int32),
             pltpu.SMEM((n_seq, 8, lanes), jnp.int32),
             dma((n_seq,)), dma((n_seq,)),
-            dma((pieces,)), dma((pieces,)),
-            dma((pieces,)), dma((pieces,)),
+            dma((pieces, CHUNKS)), dma((pieces, CHUNKS)),
+            dma((pieces, CHUNKS)), dma((pieces, CHUNKS)),
             dma((4,)), dma((4,)),
             dma((n_seq,)), dma((n_seq,)),
-            dma((5,)), dma((4,)),
+            dma((4,)), dma((4,)),
+            dma((CHUNKS,)), dma((CHUNKS,)), dma((2, features // local_width)),
         ],
         compiler_params=pltpu.CompilerParams(
             collective_id=0, has_side_effects=True, vmem_limit_bytes=58 * 2**20
@@ -311,13 +406,7 @@
         ),
         name="flow",
     )(tokens.reshape(rows, features), w_query, w_out, neighbour_kv, places)
-    terms = [
-        lax.reduce_precision(
-            jnp.dot(context[dx], w, preferred_element_type=jnp.float32), exponent_bits=8, mantissa_bits=7
-        )
-        for dx, w in enumerate([w_out, w_out_other])
-    ]
-    return (terms[0] + terms[1]).astype(bf16).reshape(local_seqs, local_span, w_out.shape[1])
+    return crossed.reshape(local_seqs, local_span, w_out.shape[1])
 
 
 def solution(mesh):

time: 443 us -> 383 us (0.86)
  Pallas kernels: 410 us -> 371 us
  matrix products: 31.3 us -> 0 us
  local copies, waits for them, and re-layouts: 0.8 us -> 8.68 us
    pallas_call x1, Pallas kernels: 410 us -> 371 us  [spread_body(): pl.pallas_call(functools.partial(flow_kernel, n_seq, n_head), out_shape=[...]
    dot_general x2 -> x0, matrix products: 31.3 us -> none  [spread_body(): jnp.dot(context[dx], w, preferred_element_type=jnp.float32)]
    unnamed x2 -> x1, local copies, waits for them, and re-layouts: 0.01 us -> 7.89 us
where the time goes in v3:
time: 383 us; the launch traced here: 381 us
  Pallas kernels  371 us (97%)
  local copies, waits for them, and re-layouts  8.68 us (2%)
    pallas_call x1, Pallas kernels, spread_body(): pl.pallas_call(functools.partial(flow_kernel, n_seq, n_head), out_shape=[...  371 us
    unnamed x1, local copies, waits for them, and re-layouts  7.89 us

profile of v3, /device:TPU:0, one launch (start us, length us, event | category | flops | bytes accessed | tf_op | source)
XLA Modules:
  0.0 380.5 jit_solution(2431006217066660247)
XLA Ops:
  0.0 0.7 multiply_add_fusion
  0.7 0.1 copy.8
  0.8 0.1 add.16
  0.9 0.6 pad.4.lists
  1.5 371.1 %flow.1 = (bf16[1024,4096]{1,0:T(8,128)(2,1)}, bf16[1024,4096]{1,0:T(8,128)(2,1)}) custom-call(bf16[1024,4096]{1,0:T(8,128)(2,1)} %bitcast.3, bf16[4096,1024]{1,0:T(8,128)(2,1)} %w_query.1, bf16[1024,4096]{1,0:T(8,128)(2,1)} %w_out.1, bf16[16,2,128,1024]{3,2,1,0:T(8,128)(2,1)} %kv.1, s32[8,128]{1,0:T(8,128)} %pad.4.lists), custom_call_target="tpu_custom_call" | custom-call | flops 17179869184 | bytes 67108864 | tf_op jit(solution)/shard_map/flow/pallas_call | solution.py:374
  372.6 7.9 %copy.10 = bf16[2,512,4096]{2,1,0:T(8,128)(2,1)} copy(bf16[2,512,4096]{2,1,0:T(8,128)(2,1)} %bitcast.2) | data formatting | bytes 16777216

commit v4 on v3

--- a/solution.py
+++ b/solution.py
@@ -61,10 +61,10 @@
 
 def flow_kernel(
     n_seq, n_head, tokens, w_query, w_out, kv, lists,
-    crossed, w_out_other,
-    context, store, q_in, q_out, c_out, normed, wq_own, wq_other, lists_in, picks,
+    normed, w_out_other,
+    context, store, q_in, q_out, c_out, wq_own, wq_other, lists_in, picks,
     kv_send, kv_recv, q_send, q_recv, c_send, c_recv, w_send, w_recv, l_send, l_recv, local, token_sem,
-    own_sem, out_sem, load_sem,
+    own_sem, load_sem,
 ):
     s = lax.axis_index("seq")
     x = lax.axis_index("head")
@@ -132,10 +132,6 @@
         return pltpu.make_async_copy(
             c_out.at[0, span], context.at[0, span, cols(s)], own_sem.at[c]
         )
-
-    def out_copy(c):
-        span = chunk_span(c)
-        return pltpu.make_async_copy(normed.at[span], crossed.at[span], out_sem.at[c])
 
     local_width = w_out.shape[0]
     out_tiles = features // local_width
@@ -308,7 +304,6 @@
             return carry
 
         lax.fori_loop(0, out_tiles, tile, 0)
-        out_copy(c).start()
 
     def turn(c, carry):
         @pl.when(c < CHUNKS)
@@ -354,8 +349,6 @@
         return carry
 
     lax.fori_loop(0, (pieces - 1) * CHUNKS, drain, 0)
-    for c in range(CHUNKS):
-        out_copy(c).wait()
 
 
 def spread_body(n_seq, n_head, tokens, w_query, w_out, neighbour_kv, shard_lists, slot_lists):
@@ -374,18 +367,17 @@
     crossed, _ = pl.pallas_call(
         functools.partial(flow_kernel, n_seq, n_head),
         out_shape=[
-            jax.ShapeDtypeStruct((rows, w_out.shape[1]), bf16),
+            pltpu.VMEM((rows, w_out.shape[1]), bf16),
             jax.ShapeDtypeStruct(w_out.shape, bf16),
         ],
         in_specs=[anywhere] * 4 + [pl.BlockSpec(memory_space=pltpu.VMEM)],
-        out_specs=[anywhere] * 2,
+        out_specs=[pl.BlockSpec(memory_space=pltpu.VMEM), anywhere],
         scratch_shapes=[
             pltpu.VMEM((n_head, rows, local_width), bf16),
             pltpu.VMEM((n_seq * count, 2, length, width), bf16),
             pltpu.VMEM((pieces, rows, width), bf16),
             pltpu.VMEM((pieces, rows, width), bf16),
             pltpu.VMEM((pieces, rows, width), bf16),
-            pltpu.VMEM((rows, features), bf16),
             pltpu.VMEM((features, local_width), bf16),
             pltpu.VMEM((features, local_width), bf16),
             pltpu.VMEM((n_seq, 8, lanes), jnp.int32),
@@ -396,10 +388,10 @@
             dma((4,)), dma((4,)),
             dma((n_seq,)), dma((n_seq,)),
             dma((4,)), dma((4,)),
-            dma((CHUNKS,)), dma((CHUNKS,)), dma((2, features // local_width)),
+            dma((CHUNKS,)), dma((2, features // local_width)),
         ],
         compiler_params=pltpu.CompilerParams(
-            collective_id=0, has_side_effects=True, vmem_limit_bytes=58 * 2**20
+            collective_id=0, has_side_effects=True, vmem_limit_bytes=48 * 2**20
         ),
         cost_estimate=pl.CostEstimate(
             flops=2 * rows * features * local_width * n_head, bytes_accessed=2**26, transcendentals=2**22

time: 383 us -> 378 us (0.987)
  local copies, waits for them, and re-layouts: 8.68 us -> 4.2 us
    unnamed x1, local copies, waits for them, and re-layouts: 7.89 us -> 3.4 us
where the time goes in v4:
time: 378 us; the launch traced here: 375 us
  Pallas kernels  370 us (98%)
  local copies, waits for them, and re-layouts  4.2 us (1%)
    pallas_call x1, Pallas kernels, spread_body(): pl.pallas_call(functools.partial(flow_kernel, n_seq, n_head), out_shape=[...  370 us

profile of v4, /device:TPU:0, one launch (start us, length us, event | category | flops | bytes accessed | tf_op | source)
XLA Modules:
  0.0 375.1 jit_solution(1518255858955701831)
XLA Ops:
  0.0 0.7 multiply_add_fusion
  0.7 0.1 copy.8
  0.8 0.1 add.16
  0.9 0.6 pad.4.lists
  1.5 370.2 %flow.1 = (bf16[1024,4096]{1,0:T(8,128)(2,1)S(1)}, bf16[1024,4096]{1,0:T(8,128)(2,1)}) custom-call(bf16[1024,4096]{1,0:T(8,128)(2,1)} %bitcast.3, bf16[4096,1024]{1,0:T(8,128)(2,1)} %w_query.1, bf16[1024,4096]{1,0:T(8,128)(2,1)} %w_out.1, bf16[16,2,128,1024]{3,2,1,0:T(8,128)(2,1)} %kv.1, s32[8,128]{1,0:T(8,128)} %pad.4.lists), custom_call_target="tpu_custom_call" | custom-call | flops 17179869184 | bytes 67108864 | tf_op jit(solution)/shard_map/flow/pallas_call | solution.py:367
  371.7 3.4 copy.10
